TPU v7x, 32 devices: a whole 2x2x4 slice. The times are simulated.
32 devices in a mesh: wide: 32 (over z, y, x, core).
Axes of the slice: x: 2, y: 2, z: 4, core: 2. Of those that a mesh axis runs over, the one named last changes fastest.
Arguments:
- tokens: bfloat16 [64, 512, 768], P('wide'), may hold values from -6 to 6
- segments: int32 [64, 512], P('wide'), may hold values from 0 to 7, never falling along the last dimension, each value on 1 to 128 neighbouring positions
- pairing: int32 [512, 2], replicated, may hold values from 0 to 511, as said below
- pair_weight: float32 [512], replicated, may hold values from 0.2 to 6
- triple_weight: bfloat16 [768, 2304], replicated, may hold values from -0.21875 to 0.21875
- query_bias: float32 [768], replicated, may hold values from -3 to 3
- value_bias: float32 [768], replicated, may hold values from -3 to 3
- mixer_weight: bfloat16 [768, 768], replicated, may hold values from -1.75 to 1.75
- mixer_bias: float32 [768], replicated, may hold values from -3 to 3
- norm_gain: float32 [768], replicated, may hold values from 0.5 to 1.5
- norm_shift: float32 [768], replicated, may hold values from -2 to 2
- expand_weight: bfloat16 [768, 3072], replicated, may hold values from -0.21875 to 0.21875
- expand_bias: float32 [3072], replicated, may hold values from -3 to 3
- shrink_weight: bfloat16 [3072, 768], replicated, may hold values from -0.109375 to 0.109375
- shrink_bias: float32 [768], replicated, may hold values from -3 to 3
- final_gain: float32 [768], replicated, may hold values from 0.5 to 1.5
- final_shift: float32 [768], replicated, may hold values from -0.6 to 0.6
Outputs:
- loss: float32 [], replicated
- layer_output: bfloat16 [64, 512, 768], P('wide')
- token_grad: float32 [64, 512, 768], P('wide')
- triple_weight_grad: float32 [768, 2304], replicated
- query_bias_grad: float32 [768], replicated
- value_bias_grad: float32 [768], replicated
- mixer_weight_grad: float32 [768, 768], replicated
- mixer_bias_grad: float32 [768], replicated
- norm_gain_grad: float32 [768], replicated
- norm_shift_grad: float32 [768], replicated
- expand_weight_grad: float32 [768, 3072], replicated
- expand_bias_grad: float32 [3072], replicated
- shrink_weight_grad: float32 [3072, 768], replicated
- shrink_bias_grad: float32 [768], replicated
- final_gain_grad: float32 [768], replicated
- final_shift_grad: float32 [768], replicated
Inputs may be any that keep to these rules, and one draw needn't show every extreme that they name: In each row the segment numbers never fall, and each of the 8 segments holds 1 to 128 tokens. `pairing`: each of the two columns names every segment number exactly once.
All inputs are finite; a program needn't handle non-finite values.
Results may differ from a plain program's by a relative error of at most 0.01.
Values may be sent and summed in bfloat16 or wider, within the bound.
No kernel may reach another device: no remote copies, remote signals or barrier semaphores. Data moves between devices by JAX's collectives and lax.ppermute only.
A program may use at most 192 MiB of HBM per device.

v0:
```python
import jax
import jax.numpy as jnp
from jax import lax
from jax.sharding import PartitionSpec as P

HEADS = 12
HEAD_DIM = 64
SEG_ROW = 8


highest = lax.Precision.HIGHEST
temper = 0.05


def prefixes(width):
    return (width // 12, width // 6, width // 3, 2 * width // 3, width)


def norm_forward(value, gain, shift):
    centre = value - jnp.mean(value, axis=-1, keepdims=True)
    inverse = lax.rsqrt(jnp.mean(centre * centre, axis=-1, keepdims=True) + 1e-05)
    scaled = centre * inverse
    return (scaled * gain + shift, scaled, inverse)


def norm_backward(grad, scaled, inverse, gain):
    inner = grad * gain
    back = inverse * (
        inner
        - jnp.mean(inner, axis=-1, keepdims=True)
        - scaled * jnp.mean(inner * scaled, axis=-1, keepdims=True)
    )
    return (back, jnp.sum(grad * scaled, axis=0), jnp.sum(grad, axis=0))


def row_scores(query, keys, row_seg):
    scores = jnp.einsum("qhd,khd->hqk", query, keys, preferred_element_type=jnp.float32) * 0.125
    mask = row_seg[:, None] == row_seg[None, :]
    return jnp.where(mask[None], scores, -1e30)


def attend_row(items):
    query, keys, values, row_seg = items
    scores = row_scores(query, keys, row_seg)
    top = jnp.max(scores, axis=-1, keepdims=True)
    expo = jnp.exp(scores - top)
    total = jnp.sum(expo, axis=-1, keepdims=True)
    probs = expo / total
    mixed = jnp.einsum(
        "hqk,khd->qhd", probs.astype(jnp.bfloat16), values, preferred_element_type=jnp.float32
    )
    return (mixed.astype(jnp.bfloat16), top + jnp.log(total))


def attend_back(items):
    query, keys, values, row_seg, spread, grad_out = items
    probs = jnp.exp(row_scores(query, keys, row_seg) - spread)
    weights = probs.astype(jnp.bfloat16)
    dprobs = jnp.einsum("qhd,khd->hqk", grad_out, values, preferred_element_type=jnp.float32)
    dvalues = jnp.einsum("hqk,qhd->khd", weights, grad_out, preferred_element_type=jnp.float32)
    dscores = (probs * (dprobs - jnp.sum(dprobs * probs, axis=-1, keepdims=True))).astype(
        jnp.bfloat16
    )
    dquery = jnp.einsum("hqk,khd->qhd", dscores, keys, preferred_element_type=jnp.float32) * 0.125
    dkeys = jnp.einsum("hqk,qhd->khd", dscores, query, preferred_element_type=jnp.float32) * 0.125
    return (dquery.astype(jnp.bfloat16), dkeys.astype(jnp.bfloat16), dvalues.astype(jnp.bfloat16))


def unit_rows(block):
    inverse = lax.rsqrt(jnp.sum(block * block, axis=1, keepdims=True) + 1e-06)
    return (block * inverse, inverse)


def unit_back(grad, unit, inverse):
    return inverse * (grad - unit * jnp.sum(grad * unit, axis=1, keepdims=True))


def on_device(
    tokens,
    segments,
    pairing,
    pair_weight,
    triple_weight,
    query_bias,
    value_bias,
    mixer_weight,
    mixer_bias,
    norm_gain,
    norm_shift,
    expand_weight,
    expand_bias,
    shrink_weight,
    shrink_bias,
    final_gain,
    final_shift,
):
    rows, length, width = tokens.shape
    flat = tokens.reshape(rows * length, width)

    def shaped(tensor):
        return tensor.reshape(rows, length, HEADS, HEAD_DIM)

    mixed = jnp.dot(flat, triple_weight, preferred_element_type=jnp.float32)
    query = (mixed[:, :width] + query_bias).astype(jnp.bfloat16)
    keys = mixed[:, width : 2 * width].astype(jnp.bfloat16)
    values = (mixed[:, 2 * width :] + value_bias).astype(jnp.bfloat16)
    attended, spread = lax.map(attend_row, (shaped(query), shaped(keys), shaped(values), segments))
    attended = attended.reshape(rows * length, width)
    branch = jnp.dot(attended, mixer_weight, preferred_element_type=jnp.float32) + mixer_bias
    first, scaled_a, inverse_a = norm_forward(
        flat.astype(jnp.float32) + branch, norm_gain, norm_shift
    )
    first_low = first.astype(jnp.bfloat16)
    expanded = jnp.dot(first_low, expand_weight, preferred_element_type=jnp.float32) + expand_bias
    active = jax.nn.gelu(expanded, approximate=False).astype(jnp.bfloat16)
    shrunk = jnp.dot(active, shrink_weight, preferred_element_type=jnp.float32) + shrink_bias
    final, scaled_b, inverse_b = norm_forward(first + shrunk, final_gain, final_shift)
    member = (segments[:, None, :] == jnp.arange(SEG_ROW, dtype=jnp.int32)[None, :, None]).astype(
        jnp.float32
    )
    counts = jnp.sum(member, axis=2, keepdims=True)
    pooled = (
        jnp.einsum("rsl,rld->rsd", member, final.reshape(rows, length, width), precision=highest)
        / counts
    )
    table = lax.all_gather(
        pooled.reshape(rows * SEG_ROW, width).astype(jnp.bfloat16), "wide", axis=0, tiled=True
    ).astype(jnp.float32)
    pair_count = pairing.shape[0]
    share = pair_count // lax.axis_size("wide")
    start = lax.axis_index("wide") * share
    owned = lax.dynamic_slice_in_dim(pairing, start, share, 0)
    own_weight = lax.dynamic_slice_in_dim(pair_weight, start, share, 0)
    anchors = jnp.take(table, owned[:, 0], axis=0)
    positives = jnp.take(table, pairing[:, 1], axis=0)
    pair_ids = jnp.arange(pair_count, dtype=jnp.int32)
    columns = start + jnp.arange(share, dtype=jnp.int32)
    target = (columns[:, None] == pair_ids[None, :]).astype(jnp.float32)
    loss_part = jnp.zeros((), jnp.float32)
    grad_anchor = jnp.zeros_like(anchors)
    grad_positive = jnp.zeros_like(positives)
    spread_list = []
    right_list = []
    for cut in prefixes(width):
        left, left_inv = unit_rows(anchors[:, :cut])
        right, right_inv = unit_rows(positives[:, :cut])
        right_list.append(right)
        sims = jnp.dot(left, right.T, precision=highest) / temper
        top = jnp.max(sims, axis=1, keepdims=True)
        expo = jnp.exp(sims - top)
        total = jnp.sum(expo, axis=1, keepdims=True)
        spread_now = top[:, 0] + jnp.log(total[:, 0])
        spread_list.append(spread_now)
        loss_part = loss_part + jnp.sum(own_weight * (spread_now - jnp.sum(sims * target, axis=1)))
        dsims = own_weight[:, None] * (expo / total - target)
        dleft = jnp.dot(dsims, right, precision=highest) / temper
        dright = jnp.dot(dsims.T, left, precision=highest) / temper
        grad_anchor = grad_anchor.at[:, :cut].add(unit_back(dleft, left, left_inv))
        grad_positive = grad_positive.at[:, :cut].add(unit_back(dright, right, right_inv))
    loss_sum = lax.psum(loss_part, "wide")
    grad_table = (
        jnp.zeros(table.shape, jnp.float32)
        .at[owned[:, 0]]
        .add(grad_anchor)
        .at[pairing[:, 1]]
        .add(grad_positive)
    )
    dpooled = lax.psum_scatter(grad_table, "wide", scatter_dimension=0, tiled=True)
    dfinal = jnp.einsum(
        "rsl,rsd->rld", member, dpooled.reshape(rows, SEG_ROW, width) / counts, precision=highest
    ).reshape(rows * length, width)
    dsecond, dgain_b, dshift_b = norm_backward(dfinal, scaled_b, inverse_b, final_gain)
    dshrunk = dsecond.astype(jnp.bfloat16)
    dshrink_w = jnp.dot(active.T, dshrunk, preferred_element_type=jnp.float32)
    dshrink_b = jnp.sum(dshrunk.astype(jnp.float32), axis=0)
    dactive = jnp.dot(dshrunk, shrink_weight.T, preferred_element_type=jnp.float32)
    normal_cdf = 0.5 * (1.0 + lax.erf(expanded * 0.7071067811865476))
    normal_pdf = jnp.exp(-0.5 * expanded * expanded) * 0.3989422804014327
    dexpanded = (dactive * (normal_cdf + expanded * normal_pdf)).astype(jnp.bfloat16)
    dexpand_w = jnp.dot(first_low.T, dexpanded, preferred_element_type=jnp.float32)
    dexpand_b = jnp.sum(dexpanded.astype(jnp.float32), axis=0)
    dfirst = dsecond + jnp.dot(dexpanded, expand_weight.T, preferred_element_type=jnp.float32)
    dbranch, dgain_a, dshift_a = norm_backward(dfirst, scaled_a, inverse_a, norm_gain)
    dbranch_low = dbranch.astype(jnp.bfloat16)
    dmixer_w = jnp.dot(attended.T, dbranch_low, preferred_element_type=jnp.float32)
    dmixer_b = jnp.sum(dbranch_low.astype(jnp.float32), axis=0)
    dattended = jnp.dot(dbranch_low, mixer_weight.T, preferred_element_type=jnp.float32).astype(
        jnp.bfloat16
    )
    dquery, dkeys, dvalues = lax.map(
        attend_back,
        (shaped(query), shaped(keys), shaped(values), segments, spread, shaped(dattended)),
    )
    dquery = dquery.reshape(rows * length, width)
    dvalues = dvalues.reshape(rows * length, width)
    dmixed = jnp.concatenate([dquery, dkeys.reshape(rows * length, width), dvalues], axis=1)
    dtriple = jnp.dot(flat.T, dmixed, preferred_element_type=jnp.float32)
    dquery_b = jnp.sum(dquery.astype(jnp.float32), axis=0)
    dvalue_b = jnp.sum(dvalues.astype(jnp.float32), axis=0)
    token_grad = dbranch + jnp.dot(dmixed, triple_weight.T, preferred_element_type=jnp.float32)
    summed = lax.psum(
        (
            dtriple,
            dquery_b,
            dvalue_b,
            dmixer_w,
            dmixer_b,
            dgain_a,
            dshift_a,
            dexpand_w,
            dexpand_b,
            dshrink_w,
            dshrink_b,
            dgain_b,
            dshift_b,
        ),
        "wide",
    )
    loss = loss_sum / pair_count
    return (
        loss,
        final.reshape(rows, length, width).astype(jnp.bfloat16),
        token_grad.reshape(rows, length, width),
        summed[0],
        summed[1],
        summed[2],
        summed[3],
        summed[4],
        summed[5],
        summed[6],
        summed[7],
        summed[8],
        summed[9],
        summed[10],
        summed[11],
        summed[12],
    )


def solution(mesh):
    return jax.shard_map(
        on_device,
        mesh=mesh,
        in_specs=(
            P("wide", None, None),
            P("wide", None),
            P(),
            P(),
            P(),
            P(),
            P(),
            P(),
            P(),
            P(),
            P(),
            P(),
            P(),
            P(),
            P(),
            P(),
            P(),
        ),
        out_specs=(
            P(),
            P("wide", None, None),
            P("wide", None, None),
            P(),
            P(),
            P(),
            P(),
            P(),
            P(),
            P(),
            P(),
            P(),
            P(),
            P(),
            P(),
            P(),
        ),
        check_vma=False,
    )
```

profile of v0, /device:TPU:0, one launch (start us, length us, event | category | flops | bytes accessed | tf_op | source)
XLA Modules:
  0.0 930.0 jit_solution(10387454160880593511)
XLA Ops:
  14.3 5.2 fusion.169
  25.8 3.8 reshape.558
  35.1 3.8 reshape.559
  44.4 3.8 reshape.557
  52.5 27.2 %while.38 = (s32[]{:T(128)}, bf16[2,512,12,64]{1,3,2,0:T(8,128)(2,1)}, f32[2,12,512,1]{2,1,3,0:T(8,128)}, bf16[2,512,12,64]{1,3,2,0:T(8,128)(2,1)}, s32[2,512]{1...) while((s32[]{:T(128)}, ...), condition=%wide.region_3.4_spmd, body=%wide.region_0.3_spmd.sunk | while | flops 843704320 | bytes 43614392 | solution.py:107
  59.9 5.5 fusion.210
  73.4 5.5 fusion.210
  87.8 34.5 %fusion.59 = (bf16[1024,3072]{1,0:T(8,128)(2,1)S(1)}, f32[1024,3072]{1,0:T(8,128)}) fusion(f32[3072]{0:T(1024)S(1)} %copy-done.56, bf16[768,3072]{1,0:T(8,128)(2,1)S(1)} %bitcast.207, f32[1024,768]{1,0:T(8,128)S(1)} %get-tuple-element.412, f32[768]{0:T(1024)S(1)} %copy-done.32, f32[768]{0:T(1024)S(1)} %copy-done.26, f32[1024]{0:T(1024)S(1)} %add_rsqrt_fusion.1, ...), kind=kOutput, calls=%fused_computation.72 | convolution fusion | flops 5043388416 | bytes 26765312 | tf_op jit(solution)/shard_map/dot_general | solution.py:114
  122.4 5.5 fusion.163
  130.8 45.3 %all_gather.3 = bf16[512,768]{1,0:T(8,128)(2,1)S(1)} all-gather(bf16[16,768]{1,0:T(8,128)(2,1)S(1)} %fusion.88), channel_id=1, replica_groups=mesh['wide'=32] {'wide'}, dimensions={0}, use_global_device_ids=true | all-gather | bytes 811008 | tf_op jit(solution)/shard_map/all_gather | solution.py:126
  184.7 4.9 gather_fusion.1
  230.8 7.6 scatter_fusion
  238.5 93.3 %reduce-scatter.2.cloned.1.call-done = f32[16,768]{1,0:T(8,128)} async-done(((f32[512,768]{1,0:T(8,128)}), f32[16,768]{1,0:T(8,128)}) %reduce-scatter.2.cloned.1.call-update) | async-done | bytes 49168 | tf_op jit(solution)/shard_map/reduce_scatter | solution.py:168
  338.6 7.8 fusion.143
  346.4 12.4 %convert_reduce_fusion = (f32[3072]{0:T(1024)}, bf16[1024,3072]{1,0:T(8,128)(2,1)S(1)}) fusion(f32[1024,3072]{1,0:T(8,128)} %get-tuple-element.414, f32[3072]{0:T(1024)S(1)} %copy-done.57, bf16[3072,768]{1,0:T(8,128)(2,1)S(1)} %bitcast.205, f32[1024,768]{1,0:T(8,128)S(1)} %get-tuple-element.387), kind=kOutput, calls=%fused_computation.79 | convolution fusion | flops 4873516032 | bytes 26763264 | tf_op jit(solution)/shard_map/dot_general | solution.py:176
  358.9 6.5 multiply_reduce_fusion.1
  365.4 8.5 fusion.157
  383.6 3.8 reshape.564
  394.3 53.6 %while.39 = (s32[]{:T(128)}, bf16[2,512,12,64]{1,3,2,0:T(8,128)(2,1)}, bf16[2,512,12,64]{1,3,2,0:T(8,128)(2,1)}, bf16[2,512,12,64]{1,3,2,0:T(8,128)(2,1)}, bf16[...) while((s32[]{:T(128)}, ...), condition=%wide.region_63.64_spmd, body=%wide.region_61.63_spmd.sunk | while | flops 2062673920 | bytes 153816432 | solution.py:190
  398.7 3.9 fusion.222
  402.6 6.9 multiply_reduce_fusion.34
  409.5 7.1 multiply_convert_fusion.4
  425.4 3.9 fusion.222
  429.3 6.9 multiply_reduce_fusion.34
  436.2 7.1 multiply_convert_fusion.4
  459.7 5.8 convolution_bitcast_fusion
  476.7 44.0 %all-reduce.2 = (f32[]{:T(128)}, f32[768]{0:T(1024)}, f32[768]{0:T(1024)}, f32[768]{0:T(1024)}, f32[768]{0:T(1024)}, /*index=5*/f32[768]{0:T(1024)}, f32[3072]{0...) all-reduce(f32[]{:T(128)S(6)} %add.401, ...), channel_id=1, replica_groups=mesh['wide'=32] {'wide'}, use_global_device_ids=true, to_apply=%region_39.40 | all-reduce | flops 9217 | bytes 73736 | tf_op jit(solution)/shard_map/psum | solution.py:160
  521.4 8.3 convolution_add_fusion.1
  529.7 368.2 %all-reduce.6.cloned.1.call-done = (f32[768,2304]{0,1:T(8,128)}, f32[768,768]{1,0:T(8,128)}, f32[768,3072]{1,0:T(8,128)}, f32[3072,768]{1,0:T(8,128)}) async-done(((f32[768,2304]{0,1:T(8,128)}, f32[768,768]{1,0:T(8,128)}, f32[768,3072]{1,0:T(8,128)}, f32[3072,768]{1,0:T(8,128)}), (f32[768,2304]{0,1:T(8,128)}, f32[768,768]{1,0:T(8,128)}, f32[768,3072]{1,0:T(8,128)}, ...) | async-done | bytes 28311568 | tf_op jit(solution)/shard_map/psum | solution.py:201
  897.9 8.0 copy.69
  909.3 8.8 copy.122
  918.0 3.7 copy.123
  (316 shorter events, 168.4 us)
Async XLA Ops:
  7.2 7.1 copy-start
  7.2 324.5 %reduce-scatter.2.cloned.1.call-start = ((), (), s32[]{:S(2)}) async-start(), calls=%async_computation.1 | async-start | bytes 1622016 | tf_op jit(solution)/shard_map/reduce_scatter | solution.py:168
  83.4 39.0 %slice-start.3 = ((s8[4718592]{0:T(1024)(128)(4,1)}), s8[4194304]{0:T(1024)(128)(4,1)S(1)}, s32[]{:S(2)}) async-start(s8[4718592]{0:T(1024)(128)(4,1)} %bitcast.202), calls=%async_computation.6 | async-start | bytes 8388608
  85.2 37.2 %copy-start.6 = (f32[1024,768]{1,0:T(8,128)}, f32[1024,768]{1,0:T(8,128)S(1)}, u32[]{:S(2)}) copy-start(f32[1024,768]{1,0:T(8,128)S(1)} %get-tuple-element.412) | copy-start | bytes 9437188
  87.8 34.6 %slice-start.4 = ((s8[4718592]{0:T(1024)(128)(4,1)}), s8[524288]{0:T(1024)(128)(4,1)S(1)}, s32[]{:S(2)}) async-start(s8[4718592]{0:T(1024)(128)(4,1)} %bitcast.202), calls=%async_computation.7 | async-start | bytes 1048576
  87.8 34.6 %copy-start.59 = (f32[768]{0:T(1024)S(1)}, f32[768]{0:T(1024)}, u32[]{:S(2)}) copy-start(f32[768]{0:T(1024)} %param.59) | copy-start | bytes 9220
  129.6 47.8 %copy-start.8 = (f32[1024,768]{1,0:T(8,128)}, f32[1024,768]{1,0:T(8,128)S(1)}, u32[]{:S(2)}) copy-start(f32[1024,768]{1,0:T(8,128)S(1)} %multiply_add_fusion) | copy-start | bytes 9437188
  129.6 47.7 %copy-start.35 = (s32[512,1]{0,1:T(1,128)S(1)}, s32[512,1]{0,1:T(1,128)}, u32[]{:S(2)}) copy-start(s32[512,1]{0,1:T(1,128)} %get-tuple-element.396) | copy-start | bytes 6148
  129.6 47.7 %copy-start.51 = (s32[16]{0:T(128)S(1)}, s32[16]{0:T(128)}, u32[]{:S(2)}) copy-start(s32[16]{0:T(128)} %fusion.146) | copy-start | bytes 196
  194.7 16.6 %copy-start.39 = (f32[16]{0:T(128)}, f32[16]{0:T(128)S(1)}, u32[]{:S(2)}) copy-start(f32[16]{0:T(128)S(1)} %add_rsqrt_fusion.7) | copy-start | bytes 196
  194.7 15.4 %copy-start.41 = (f32[16]{0:T(128)}, f32[16]{0:T(128)S(1)}, u32[]{:S(2)}) copy-start(f32[16]{0:T(128)S(1)} %add_rsqrt_fusion.8) | copy-start | bytes 196
  194.8 14.6 %copy-start.40 = (f32[16]{0:T(128)}, f32[16]{0:T(128)S(1)}, u32[]{:S(2)}) copy-start(f32[16]{0:T(128)S(1)} %add_rsqrt_fusion.9) | copy-start | bytes 196
  194.8 14.0 %copy-start.42 = (f32[16]{0:T(128)}, f32[16]{0:T(128)S(1)}, u32[]{:S(2)}) copy-start(f32[16]{0:T(128)S(1)} %add_rsqrt_fusion.10) | copy-start | bytes 196
  238.4 659.5 %all-reduce.6.cloned.1.call-start = ((), (), s32[]{:S(2)}) async-start(), calls=%async_computation.2 | async-start | bytes 56623104 | tf_op jit(solution)/shard_map/psum | solution.py:201
  331.7 6.8 slice-start.11
  336.6 9.8 %slice-start.5 = ((s8[4718592]{0:T(1024)(128)(4,1)}), s8[4194304]{0:T(1024)(128)(4,1)S(1)}, s32[]{:S(2)}) async-start(s8[4718592]{0:T(1024)(128)(4,1)} %bitcast.204), calls=%async_computation.8 | async-start | bytes 8388608
  338.5 7.9 slice-start.6
  338.5 7.9 copy-start.57
  338.5 20.3 %slice-start.9 = ((s8[4718592]{0:T(1024)(128)(4,1)}), s8[4194304]{0:T(1024)(128)(4,1)S(1)}, s32[]{:S(2)}) async-start(s8[4718592]{0:T(1024)(128)(4,1)} %bitcast.208), calls=%async_computation.12 | async-start | bytes 8388608
  346.4 12.5 %copy-start.7 = (f32[1024,768]{1,0:T(8,128)S(1)}, f32[1024,768]{1,0:T(8,128)}, u32[]{:S(2)}) copy-start(f32[1024,768]{1,0:T(8,128)} %copy-done.6) | copy-start | bytes 9437188
  346.4 12.5 %copy-start.27 = (f32[768]{0:T(1024)S(1)}, f32[768]{0:T(1024)}, u32[]{:S(2)}) copy-start(f32[768]{0:T(1024)} %param.54) | copy-start | bytes 9220
  346.4 12.5 %slice-start.10 = ((s8[4718592]{0:T(1024)(128)(4,1)}), s8[524288]{0:T(1024)(128)(4,1)S(1)}, s32[]{:S(2)}) async-start(s8[4718592]{0:T(1024)(128)(4,1)} %bitcast.208), calls=%async_computation.13 | async-start | bytes 1048576
  358.9 6.5 copy-start.33
  409.5 7.1 copy-start.1
  409.5 7.1 copy-start.14
  436.2 7.1 copy-start.1
  436.2 7.1 copy-start.14
  465.5 11.2 %copy-start.36 = (f32[768]{0:T(1024)S(1)}, f32[768]{0:T(1024)}, u32[]{:S(2)}) copy-start(f32[768]{0:T(1024)} %get-tuple-element.320) | copy-start | bytes 9220
  465.5 11.2 %copy-start.37 = (f32[768]{0:T(1024)S(1)}, f32[768]{0:T(1024)}, u32[]{:S(2)}) copy-start(f32[768]{0:T(1024)} %get-tuple-element.386) | copy-start | bytes 9220
  905.9 12.1 %slice-start = ((s8[9437184]{0:T(1024)(128)(4,1)}), s8[4194304]{0:T(1024)(128)(4,1)S(1)}, s32[]{:S(2)}) async-start(s8[9437184]{0:T(1024)(128)(4,1)} %bitcast.186), calls=%async_computation.3 | async-start | bytes 8388608
  909.3 8.8 slice-start.1
  909.3 8.8 slice-start.2
  (55 other events, 138.7 us)
Sparse Core Ops, SparseCore 0:
  238.5 93.1 reduce-scatter.1
  465.6 432.2 all-reduce.5
where the time goes:
time: 935 us; the launch traced here: 930 us
  waiting for transfers between devices  462 us (49%)
  matrix products  175 us (19%)
  local copies, waits for them, and re-layouts  108 us (12%)
  blocking collectives  89.4 us (10%)
  other arithmetic  75 us (8%)
  between operations  20.2 us (2%)
    psum x1, waiting for transfers between devices, on_device(): lax.psum((dtriple, dquery_b, dvalue_b, dmixer_w, dmixer_b, dgain_a, dshif...  368 us
    reduce_scatter x1, waiting for transfers between devices, on_device(): lax.psum_scatter(grad_table, 'wide', scatter_dimension=0, tiled=True)  93.3 us
    all_gather x1, blocking collectives, on_device(): lax.all_gather(pooled.reshape(rows * SEG_ROW, width).astype(jnp.bfloat16)...  45.3 us
    psum x1, blocking collectives, on_device(): loss_sum = lax.psum(loss_part, 'wide')  44 us
    dot_general x1, matrix products, on_device(): jnp.dot(first_low, expand_weight, preferred_element_type=jnp.float32)  34.5 us
    unnamed x137, local copies, waits for them, and re-layouts  30.9 us
  transfers between devices with their start and end apart: 2, of which 2 were waited for; matrix products, arithmetic and copies ran while one was open for 2% of the time, Pallas kernels for 0%

commit v1 on v0

--- a/solution.py
+++ b/solution.py
@@ -1,19 +1,235 @@
+import functools
+
 import jax
 import jax.numpy as jnp
 from jax import lax
+from jax.experimental import pallas as pl
+from jax.experimental.pallas import tpu as pltpu
 from jax.sharding import PartitionSpec as P
 
 HEADS = 12
 HEAD_DIM = 64
 SEG_ROW = 8
-
+AXIS = "wide"
+F32 = jnp.float32
+BF16 = jnp.bfloat16
 
 highest = lax.Precision.HIGHEST
-temper = 0.05
+scale = 20.0
 
 
 def prefixes(width):
     return (width // 12, width // 6, width // 3, 2 * width // 3, width)
+
+
+def dot(a, b):
+    return jnp.dot(a, b, preferred_element_type=F32)
+
+
+def dot_nt(a, b):
+    return lax.dot_general(a, b, (((1,), (1,)), ((), ())), preferred_element_type=F32)
+
+
+def window(array, low, high):
+    first, last = low // 128 * 128, -(-high // 128) * 128
+    piece = array[:, first:last]
+    if first == low and last == high:
+        return piece, first, last
+    lane = first + lax.broadcasted_iota(jnp.int32, (1, last - first), 1)
+    return jnp.where((lane >= low) & (lane < high), piece, jnp.zeros_like(piece)), first, last
+
+
+def split(value):
+    high = value.astype(BF16)
+    return high, (value - high.astype(F32)).astype(BF16)
+
+
+def flip(size, low, high):
+    return [(i, i ^ (high if i & 1 else low)) for i in range(size)]
+
+
+def bit_of(me, bit):
+    return (me // bit) % 2
+
+
+def stages(me, size):
+    out = [(flip(size, 1, 1), bit_of(me, 1))]
+    bits = [1 << k for k in range(1, size.bit_length() - 1)]
+    if len(bits) > 1:
+        a, b = bits[0], bits[1]
+        core = bit_of(me, 1)
+        one, two = bit_of(me, a), bit_of(me, b)
+        out.append((flip(size, a, b), jnp.where(core == 0, one, two)))
+        out.append((flip(size, b, a), jnp.where(core == 0, two, one)))
+        bits = bits[2:]
+    for bit in bits:
+        out.append((flip(size, bit, bit), bit_of(me, bit)))
+    return out
+
+
+def gather_rows(block, size):
+    bit = size // 2
+    while bit:
+        other = lax.ppermute(block, AXIS, flip(size, bit, bit))
+        block = jnp.concatenate([block, other], axis=0)
+        bit //= 2
+    return block
+
+
+def sum_over(value, plan):
+    for pairs, mine in plan:
+        half = value.shape[0] // 2
+        keep = lax.dynamic_slice_in_dim(value, mine * half, half, 0)
+        send = lax.dynamic_slice_in_dim(value, (1 - mine) * half, half, 0)
+        got = lax.ppermute(send, AXIS, pairs)
+        value = (keep.astype(F32) + got.astype(F32)).astype(BF16)
+    for pairs, mine in plan[::-1]:
+        got = lax.ppermute(value, AXIS, pairs)
+        value = jnp.where(
+            mine == 0,
+            jnp.concatenate([value, got], axis=0),
+            jnp.concatenate([got, value], axis=0),
+        )
+    return value.astype(F32)
+
+
+def sum_small(value, size):
+    bit = 1
+    while bit < size:
+        value = value + lax.ppermute(value, AXIS, flip(size, bit, bit))
+        bit *= 2
+    return value
+
+
+def contrast_kernel(
+    size, me_ref, gathered, own_ref, cols_ref, rows_ref, load_col_ref, load_row_ref, loss_ref, grad_ref, table, total, aim
+):
+    me = me_ref[0]
+    count, width = table.shape
+    share = own_ref.shape[0]
+    block = 128
+    levels = size.bit_length() - 1
+    for place in range(size):
+        mask = sum(((place >> k) & 1) << (levels - 1 - k) for k in range(levels))
+        owner = me ^ mask
+        table[pl.ds(pl.multiple_of(owner * share, share), share), :] = gathered[
+            place * share : (place + 1) * share, :
+        ]
+    cuts = prefixes(width)
+    spans = list(zip((0,) + cuts[:-1], cuts))
+    lane_ids = lax.broadcasted_iota(jnp.int32, (1, count), 1)
+
+    def place_pairs(i, carry):
+        partner, load = carry
+        rows = pl.ds(pl.multiple_of(i * block, block), block)
+        hit = cols_ref[rows, 0:1] == lane_ids
+        partner = partner + jnp.sum(
+            jnp.where(hit, cols_ref[rows, 1:2].astype(F32), 0.0), axis=0, keepdims=True
+        )
+        load = load + jnp.sum(jnp.where(hit, load_col_ref[rows, :], 0.0), axis=0, keepdims=True)
+        return partner, load
+
+    zero_row = jnp.zeros((1, count), F32)
+    partner_row, load_row = lax.fori_loop(0, count // block, place_pairs, (zero_row, zero_row))
+    own_ids = me * share + lax.broadcasted_iota(jnp.int32, (share, 1), 0)
+    hit = rows_ref[0:1, :] == own_ids
+    partner_own = jnp.sum(jnp.where(hit, rows_ref[1:2, :].astype(F32), 0.0), axis=1, keepdims=True)
+    load_own = jnp.sum(jnp.where(hit, load_row_ref[...], 0.0), axis=1, keepdims=True)
+
+    squares = jnp.zeros((count, 1), F32)
+    side = jnp.zeros((count, 128), F32)
+    for k, (low, high) in enumerate(spans):
+        piece, first, last = window(table, low, high)
+        wide = piece.astype(F32)
+        squares = squares + jnp.sum(wide * wide, axis=1, keepdims=True)
+        lane = lax.broadcasted_iota(jnp.int32, (1, 128), 1)
+        side = jnp.where(lane == k, squares, side)
+    upright = lax.rsqrt(jnp.transpose(side)[0:8, :] + 1e-06) * scale
+    inverse_rows = [upright[k : k + 1, :] for k in range(len(cuts))]
+
+    total[...] = jnp.zeros_like(total)
+    aim[...] = jnp.zeros_like(aim)
+
+    def add_rows(i, carry):
+        start = pl.multiple_of(i * block, block)
+        sims = jnp.zeros((block, count), F32)
+        squares = jnp.zeros((block, 1), F32)
+        row_ids = (start + lax.broadcasted_iota(jnp.int32, (block, 1), 0)).astype(F32)
+        chosen = partner_row == row_ids
+        for k, (low, high) in enumerate(spans):
+            piece, first, last = window(table.at[pl.ds(start, block), :], low, high)
+            wide = piece.astype(F32)
+            squares = squares + jnp.sum(wide * wide, axis=1, keepdims=True)
+            sims = sims + dot_nt(piece, table[:, first:last])
+            value = sims * lax.rsqrt(squares + 1e-06) * inverse_rows[k]
+            total[k : k + 1, :] += jnp.sum(jnp.exp(value - scale), axis=0, keepdims=True)
+            aim[k : k + 1, :] += jnp.sum(jnp.where(chosen, value, 0.0), axis=0, keepdims=True)
+        return carry
+
+    lax.fori_loop(0, count // block, add_rows, 0)
+
+    spreads = scale + jnp.log(total[0 : len(cuts), :])
+    gaps = jnp.sum(spreads - aim[0 : len(cuts), :], axis=0, keepdims=True)
+    loss_ref[...] = jnp.broadcast_to(
+        jnp.sum(gaps * load_row, axis=1, keepdims=True) / count, loss_ref.shape
+    )
+
+    sims = jnp.zeros((share, count), F32)
+    squares = jnp.zeros((share, 1), F32)
+    out_hit = (partner_own == lane_ids.astype(F32)).astype(F32)
+    in_hit = (partner_row == own_ids.astype(F32)).astype(F32)
+    grad_ref[...] = jnp.zeros_like(grad_ref)
+    for k, (low, high) in enumerate(spans):
+        piece, first, last = window(own_ref, low, high)
+        wide = piece.astype(F32)
+        squares = squares + jnp.sum(wide * wide, axis=1, keepdims=True)
+        inverse = lax.rsqrt(squares + 1e-06)
+        sims = sims + dot_nt(piece, table[:, first:last])
+        value = sims * inverse * inverse_rows[k]
+        spread = scale + jnp.log(jnp.sum(jnp.exp(value - scale), axis=1, keepdims=True))
+        dsims = load_own * (jnp.exp(value - spread) - out_hit) + load_row * (
+            jnp.exp(value - spreads[k : k + 1, :]) - in_hit
+        )
+        big, small = split(dsims * inverse_rows[k])
+        unit, _, last = window(own_ref, 0, high)
+        unit = unit.astype(F32) * inverse
+        dunit = dot(big, table[:, :last]) + dot(small, table[:, :last])
+        if last != high:
+            lane = lax.broadcasted_iota(jnp.int32, (1, last), 1)
+            dunit = jnp.where(lane < high, dunit, 0.0)
+        along = jnp.sum(dunit * unit, axis=1, keepdims=True)
+        grad_ref[:, :last] += inverse * (dunit - unit * along)
+
+
+def contrast(gathered, own, pairing, pair_weight, me, size):
+    share, width = own.shape
+    count = share * size
+    vmem = pl.BlockSpec(memory_space=pltpu.VMEM)
+    loss, grad = pl.pallas_call(
+        functools.partial(contrast_kernel, size),
+        out_shape=(
+            jax.ShapeDtypeStruct((8, 128), F32),
+            jax.ShapeDtypeStruct((share, width), F32),
+        ),
+        in_specs=[pl.BlockSpec(memory_space=pltpu.SMEM)] + [vmem] * 6,
+        out_specs=(vmem, vmem),
+        scratch_shapes=[
+            pltpu.VMEM((count, width), BF16),
+            pltpu.VMEM((8, count), F32),
+            pltpu.VMEM((8, count), F32),
+        ],
+        compiler_params=pltpu.CompilerParams(vmem_limit_bytes=56 * 1024 * 1024),
+        name="contrast",
+    )(
+        me.reshape(1),
+        gathered,
+        own,
+        pairing,
+        pairing.T,
+        pair_weight[:, None],
+        pair_weight[None, :],
+    )
+    return loss[0, 0], grad
 
 
 def norm_forward(value, gain, shift):
@@ -64,15 +280,6 @@
     dquery = jnp.einsum("hqk,khd->qhd", dscores, keys, preferred_element_type=jnp.float32) * 0.125
     dkeys = jnp.einsum("hqk,qhd->khd", dscores, query, preferred_element_type=jnp.float32) * 0.125
     return (dquery.astype(jnp.bfloat16), dkeys.astype(jnp.bfloat16), dvalues.astype(jnp.bfloat16))
-
-
-def unit_rows(block):
-    inverse = lax.rsqrt(jnp.sum(block * block, axis=1, keepdims=True) + 1e-06)
-    return (block * inverse, inverse)
-
-
-def unit_back(grad, unit, inverse):
-    return inverse * (grad - unit * jnp.sum(grad * unit, axis=1, keepdims=True))
 
 
 def on_device(
@@ -123,49 +330,10 @@
         jnp.einsum("rsl,rld->rsd", member, final.reshape(rows, length, width), precision=highest)
         / counts
     )
-    table = lax.all_gather(
-        pooled.reshape(rows * SEG_ROW, width).astype(jnp.bfloat16), "wide", axis=0, tiled=True
-    ).astype(jnp.float32)
-    pair_count = pairing.shape[0]
-    share = pair_count // lax.axis_size("wide")
-    start = lax.axis_index("wide") * share
-    owned = lax.dynamic_slice_in_dim(pairing, start, share, 0)
-    own_weight = lax.dynamic_slice_in_dim(pair_weight, start, share, 0)
-    anchors = jnp.take(table, owned[:, 0], axis=0)
-    positives = jnp.take(table, pairing[:, 1], axis=0)
-    pair_ids = jnp.arange(pair_count, dtype=jnp.int32)
-    columns = start + jnp.arange(share, dtype=jnp.int32)
-    target = (columns[:, None] == pair_ids[None, :]).astype(jnp.float32)
-    loss_part = jnp.zeros((), jnp.float32)
-    grad_anchor = jnp.zeros_like(anchors)
-    grad_positive = jnp.zeros_like(positives)
-    spread_list = []
-    right_list = []
-    for cut in prefixes(width):
-        left, left_inv = unit_rows(anchors[:, :cut])
-        right, right_inv = unit_rows(positives[:, :cut])
-        right_list.append(right)
-        sims = jnp.dot(left, right.T, precision=highest) / temper
-        top = jnp.max(sims, axis=1, keepdims=True)
-        expo = jnp.exp(sims - top)
-        total = jnp.sum(expo, axis=1, keepdims=True)
-        spread_now = top[:, 0] + jnp.log(total[:, 0])
-        spread_list.append(spread_now)
-        loss_part = loss_part + jnp.sum(own_weight * (spread_now - jnp.sum(sims * target, axis=1)))
-        dsims = own_weight[:, None] * (expo / total - target)
-        dleft = jnp.dot(dsims, right, precision=highest) / temper
-        dright = jnp.dot(dsims.T, left, precision=highest) / temper
-        grad_anchor = grad_anchor.at[:, :cut].add(unit_back(dleft, left, left_inv))
-        grad_positive = grad_positive.at[:, :cut].add(unit_back(dright, right, right_inv))
-    loss_sum = lax.psum(loss_part, "wide")
-    grad_table = (
-        jnp.zeros(table.shape, jnp.float32)
-        .at[owned[:, 0]]
-        .add(grad_anchor)
-        .at[pairing[:, 1]]
-        .add(grad_positive)
-    )
-    dpooled = lax.psum_scatter(grad_table, "wide", scatter_dimension=0, tiled=True)
+    size = lax.axis_size(AXIS)
+    me = lax.axis_index(AXIS)
+    own = pooled.reshape(rows * SEG_ROW, width).astype(BF16)
+    loss, dpooled = contrast(gather_rows(own, size), own, pairing, pair_weight, me, size)
     dfinal = jnp.einsum(
         "rsl,rsd->rld", member, dpooled.reshape(rows, SEG_ROW, width) / counts, precision=highest
     ).reshape(rows * length, width)
@@ -198,25 +366,32 @@
     dquery_b = jnp.sum(dquery.astype(jnp.float32), axis=0)
     dvalue_b = jnp.sum(dvalues.astype(jnp.float32), axis=0)
     token_grad = dbranch + jnp.dot(dmixed, triple_weight.T, preferred_element_type=jnp.float32)
-    summed = lax.psum(
-        (
-            dtriple,
-            dquery_b,
-            dvalue_b,
-            dmixer_w,
-            dmixer_b,
-            dgain_a,
-            dshift_a,
-            dexpand_w,
-            dexpand_b,
-            dshrink_w,
-            dshrink_b,
-            dgain_b,
-            dshift_b,
-        ),
-        "wide",
-    )
-    loss = loss_sum / pair_count
+    plan = stages(me, size)
+    small = sum_small(
+        jnp.concatenate(
+            [dquery_b, dvalue_b, dmixer_b, dgain_a, dshift_a, dexpand_b, dshrink_b, dgain_b, dshift_b]
+        ).reshape(-1, width),
+        size,
+    )
+    fan = expand_bias.shape[0] // width
+    dshrink_w = sum_over(dshrink_w.astype(BF16), plan)
+    dexpand_w = sum_over(dexpand_w.astype(BF16), plan)
+    both = sum_over(jnp.concatenate([dtriple, dmixer_w], axis=1).astype(BF16), plan)
+    summed = (
+        both[:, : 3 * width],
+        small[0],
+        small[1],
+        both[:, 3 * width :],
+        small[2],
+        small[3],
+        small[4],
+        dexpand_w,
+        small[5 : 5 + fan].reshape(-1),
+        dshrink_w,
+        small[5 + fan],
+        small[6 + fan],
+        small[7 + fan],
+    )
     return (
         loss,
         final.reshape(rows, length, width).astype(jnp.bfloat16),

time: 935 us -> 537 us (0.57)
  waiting for transfers between devices: 462 us -> 114 us
  blocking collectives: 89.4 us -> 0 us
  starting transfers between devices: 0.08 us -> 65.3 us
  matrix products: 175 us -> 155 us
  between operations: 20.2 us -> 1.93 us
    psum x1 -> x0, waiting for transfers between devices: 368 us -> none  [on_device(): lax.psum((dtriple, dquery_b, dvalue_b, dmixer_w, dmixer_b, dgain_a, dshif...]
    ppermute x0 -> x40, waiting for transfers between devices: none -> 114 us  [the longest x15 67.3 us: sum_over(): got = lax.ppermute(send, AXIS, pairs)]
    reduce_scatter x1 -> x0, waiting for transfers between devices: 93.3 us -> none  [on_device(): lax.psum_scatter(grad_table, 'wide', scatter_dimension=0, tiled=True)]
    ppermute x0 -> x40, starting transfers between devices: none -> 65.3 us  [the longest x15 29.6 us: sum_over(): got = lax.ppermute(value, AXIS, pairs)]
    all_gather x1 -> x0, blocking collectives: 45.3 us -> none  [on_device(): lax.all_gather(pooled.reshape(rows * SEG_ROW, width).astype(jnp.bfloat16)...]
    psum x1 -> x0, blocking collectives: 44 us -> none  [on_device(): loss_sum = lax.psum(loss_part, 'wide')]
    convert_element_type x1 -> x18, other arithmetic: 1.25 us -> 32.3 us  [the longest x3 22.4 us: sum_over(): return value.astype(F32)]
    scatter-add x8 -> x0, other arithmetic: 18.6 us -> none  [the longest x2 9.88 us: on_device(): grad_table = jnp.zeros(table.shape, jnp.float32).at[owned[:, 0]].add(grad...]
  transfers between devices with their start and end apart: 2 -> 40, of which waited for: 2 -> 19; matrix products, arithmetic and copies ran while one was open for 2% -> 16% of each run, Pallas kernels for 0% -> 0%
where the time goes in v1:
time: 537 us; the launch traced here: 532 us
  matrix products  155 us (29%)
  waiting for transfers between devices  114 us (21%)
  local copies, waits for them, and re-layouts  105 us (20%)
  other arithmetic  82.7 us (15%)
  starting transfers between devices  65.3 us (12%)
  Pallas kernels  7.66 us (1%)
    ppermute x15, waiting for transfers between devices, sum_over(): got = lax.ppermute(send, AXIS, pairs)  67.3 us
    dot_general x1, matrix products, on_device(): jnp.dot(first_low, expand_weight, preferred_element_type=jnp.float32)  34.5 us
    ppermute x15, waiting for transfers between devices, sum_over(): got = lax.ppermute(value, AXIS, pairs)  29.6 us
    ppermute x15, starting transfers between devices, sum_over(): got = lax.ppermute(value, AXIS, pairs)  29.6 us
    unnamed x149, local copies, waits for them, and re-layouts  24.7 us
    convert_element_type x3, other arithmetic, sum_over(): return value.astype(F32)  22.4 us
    ppermute x15, starting transfers between devices, sum_over(): got = lax.ppermute(send, AXIS, pairs)  21.1 us
    reshape x4, local copies, waits for them, and re-layouts, shaped(): return tensor.reshape(rows, length, HEADS, HEAD_DIM)  15.4 us
  transfers between devices with their start and end apart: 40, of which 19 were waited for; matrix products, arithmetic and copies ran while one was open for 16% of the time, Pallas kernels for 0%

profile of v1, /device:TPU:0, one launch (start us, length us, event | category | flops | bytes accessed | tf_op | source)
XLA Modules:
  0.0 531.7 jit_solution(16041090824015828154)
XLA Ops:
  2.7 5.2 fusion.99
  41.3 27.1 %while.26 = (s32[]{:T(128)}, bf16[2,512,12,64]{1,3,2,0:T(8,128)(2,1)}, f32[2,12,512,1]{2,1,3,0:T(8,128)}, bf16[2,512,12,64]{1,3,2,0:T(8,128)(2,1)}, s32[2,512]{1...) while((s32[]{:T(128)}, ...), condition=%wide.region_3.4_spmd, body=%wide.region_0.3_spmd.sunk | while | flops 843704320 | bytes 43614392 | solution.py:314
  48.6 5.5 %fusion.140 = bf16[2,512,12,64]{1,3,2,0:T(8,128)(2,1)} fusion(bf16[2,512,12,64]{1,3,2,0:T(8,128)(2,1)} %get-tuple-element.421, s32[]{:T(128)S(6)} %copy.148, f32[12,512,512]{1,2,0:T(8,128)S(1)} %get-tuple-element.398, f32[12,512]{1,0:T(8,128)S(1)} %fusion.139, f32[12,512]{1,0:T(8,128)S(1)} %get-tuple-element.399, pred[512,512]{0,1:T(8,128)(4,1)} %copy-done.3, ...), kind=kOutput, calls=%fused_computation.8.clone.1 | convolution fusion | flops 418775040 | bytes 14468096 | tf_op jit(solution)/shard_map/while/body/eval_jaxpr/hqk,khd->qhd/dot_general | solution.py:265
  62.1 5.5 %fusion.140 = bf16[2,512,12,64]{1,3,2,0:T(8,128)(2,1)} fusion(bf16[2,512,12,64]{1,3,2,0:T(8,128)(2,1)} %get-tuple-element.421, s32[]{:T(128)S(6)} %copy.148, f32[12,512,512]{1,2,0:T(8,128)S(1)} %get-tuple-element.398, f32[12,512]{1,0:T(8,128)S(1)} %fusion.139, f32[12,512]{1,0:T(8,128)S(1)} %get-tuple-element.399, pred[512,512]{0,1:T(8,128)(4,1)} %copy-done.3, ...), kind=kOutput, calls=%fused_computation.8.clone.1 | convolution fusion | flops 418775040 | bytes 14468096 | tf_op jit(solution)/shard_map/while/body/eval_jaxpr/hqk,khd->qhd/dot_general | solution.py:265
  76.5 34.5 %fusion.59 = (bf16[1024,3072]{1,0:T(8,128)(2,1)S(1)}, f32[1024,3072]{1,0:T(8,128)}) fusion(f32[3072]{0:T(1024)S(1)} %copy-done.55, bf16[768,3072]{1,0:T(8,128)(2,1)S(1)} %bitcast.210, f32[1024,768]{1,0:T(8,128)S(1)} %get-tuple-element.288, f32[768]{0:T(1024)S(1)} %copy-done.59, f32[768]{0:T(1024)S(1)} %copy-done.47, f32[1024]{0:T(1024)S(1)} %add_rsqrt_fusion.1, ...), kind=kOutput, calls=%fused_computation.68 | convolution fusion | flops 5043388416 | bytes 26765312 | tf_op jit(solution)/shard_map/dot_general | solution.py:321
  111.1 5.5 %fusion.98 = (f32[1024]{0:T(1024)S(1)}, f32[1024,768]{1,0:T(8,128)S(1)}) fusion(f32[768]{0:T(1024)S(1)} %copy-done.58, bf16[1024,3072]{1,0:T(8,128)(2,1)S(1)} %get-tuple-element.289, bf16[3072,768]{1,0:T(8,128)(2,1)S(1)} %bitcast.206, f32[768]{0:T(1024)S(1)} %copy-done.59, f32[768]{0:T(1024)S(1)} %copy-done.47, f32[1024]{0:T(1024)S(1)} %add_rsqrt_fusion.1, ...), kind=kOutput, calls=%fused_computation.239 | convolution fusion | flops 4837342208 | bytes 17323008 | tf_op jit(solution)/shard_map/dot_general | solution.py:323
  147.8 7.7 %contrast.1 = (f32[8,128]{1,0:T(8,128)}, f32[16,768]{1,0:T(8,128)}) custom-call(s32[1]{0:T(128)} %bitcast.19.me_ref, bf16[512,768]{1,0:T(8,128)(2,1)} %constant_dynamic-update-slice_fusion.5.gathered, bf16[16,768]{1,0:T(8,128)(2,1)} %copy-done.27, s32[512,2]{1,0:T(8,128)} %copy.117.cols_ref, s32[2,512]{1,0:T(2,128)} %bitcast.201, ...), custom_call_target="tpu_custom_call" | custom-call | tf_op jit(solution)/shard_map/contrast/pallas_call | solution.py:208
  162.7 7.1 %convolution_convert_fusion = bf16[3072,768]{1,0:T(8,128)(2,1)} fusion(bf16[1024,3072]{1,0:T(8,128)(2,1)S(1)} %bitcast.218, f32[1024,768]{1,0:T(8,128)S(1)} %get-tuple-element.268), kind=kOutput, calls=%fused_computation.93 | convolution fusion | flops 4834983936 | bytes 14155776 | tf_op jit(solution)/shard_map/dot_general | solution.py:342
  169.8 12.4 %convert_reduce_fusion = (f32[3072]{0:T(1024)}, bf16[1024,3072]{1,0:T(8,128)(2,1)S(1)}) fusion(f32[1024,3072]{1,0:T(8,128)} %get-tuple-element.290, f32[3072]{0:T(1024)S(1)} %copy-done.56, bf16[3072,768]{1,0:T(8,128)(2,1)S(1)} %bitcast.208, f32[1024,768]{1,0:T(8,128)S(1)} %get-tuple-element.268), kind=kOutput, calls=%fused_computation.75 | convolution fusion | flops 4873516032 | bytes 26763264 | tf_op jit(solution)/shard_map/dot_general | solution.py:344
  182.3 6.6 %multiply_reduce_fusion.1 = (f32[768]{0:T(1024)}, f32[1024]{0:T(1024)S(1)}, f32[1024]{0:T(1024)S(1)}, f32[768]{0:T(1024)}, f32[1024,768]{1,0:T(8,128)S(1)}) fusion(f32[1024,768]{1,0:T(8,128)S(1)} %copy-done.16, f32[1024]{0:T(1024)S(1)} %copy-done.38, f32[1024]{0:T(1024)S(1)} %copy-done.35, f32[768]{0:T(1024)S(1)} %copy-done.48, ...), kind=kOutput, calls=%fused_computation.117 | convolution fusion | flops 4839698432 | bytes 20472832 | tf_op jit(solution)/shard_map/dot_general | solution.py:350
  188.9 7.9 %convolution_convert_fusion.1 = bf16[768,3072]{1,0:T(8,128)(2,1)} fusion(bf16[1024,3072]{1,0:T(8,128)(2,1)S(1)} %get-tuple-element.297, f32[1024,768]{1,0:T(8,128)S(1)} %copy-done.16, f32[768]{0:T(1024)S(1)} %copy-done.60, f32[768]{0:T(1024)S(1)} %copy-done.48, f32[1024]{0:T(1024)S(1)} %copy-done.38, f32[1024]{0:T(1024)S(1)} %copy-done.35), kind=kOutput, calls=%fused_computation.94 | convolution fusion | flops 4838129664 | bytes 14170112 | tf_op jit(solution)/shard_map/dot_general | solution.py:348
  216.1 53.5 %while.27 = (s32[]{:T(128)}, bf16[2,512,12,64]{1,3,2,0:T(8,128)(2,1)}, bf16[2,512,12,64]{1,3,2,0:T(8,128)(2,1)}, bf16[2,512,12,64]{1,3,2,0:T(8,128)(2,1)}, bf16[...) while((s32[]{:T(128)}, ...), condition=%wide.region_15.16_spmd, body=%wide.region_13.15_spmd.sunk | while | flops 2062673920 | bytes 153816432 | solution.py:358
  224.4 6.8 %multiply_reduce_fusion.9 = (f32[12,512]{1,0:T(8,128)S(1)}, f32[12,512,512]{1,2,0:T(8,128)}) fusion(f32[12,512,512]{1,2,0:T(8,128)S(1)} %fusion.149, f32[12,512]{1,0:T(8,128)S(1)} %dynamic-slice_bitcast_fusion.2, pred[512,512]{0,1:T(8,128)(4,1)S(1)} %broadcast_compare_fusion.5, bf16[2,512,12,64]{1,3,2,0:T(8,128)(2,1)S(1)} %copy-done.8, ...), kind=kOutput, calls=%fused_computation.24.clone.1 | convolution fusion | flops 418375680 | bytes 27059200 | tf_op jit(solution)/shard_map/while/body/eval_jaxpr/qhd,khd->hqk/dot_general | solution.py:275
  231.2 7.1 %multiply_convert_fusion.4 = bf16[12,512,512]{1,2,0:T(8,128)(2,1)S(1)} fusion(f32[12,512,512]{1,2,0:T(8,128)} %get-tuple-element.410, f32[12,512,512]{1,2,0:T(8,128)S(1)} %fusion.149, f32[12,512]{1,0:T(8,128)S(1)} %get-tuple-element.411, f32[12,512]{1,0:T(8,128)S(1)} %dynamic-slice_bitcast_fusion.2, pred[512,512]{0,1:T(8,128)(4,1)S(1)} %broadcast_compare_fusion.5), kind=kLoop, calls=%fused_computation.23.clone.1 | loop fusion | flops 18874368 | bytes 31768576 | tf_op jit(solution)/shard_map/while/body/eval_jaxpr/convert_element_type | solution.py:277
  251.0 6.8 %multiply_reduce_fusion.9 = (f32[12,512]{1,0:T(8,128)S(1)}, f32[12,512,512]{1,2,0:T(8,128)}) fusion(f32[12,512,512]{1,2,0:T(8,128)S(1)} %fusion.149, f32[12,512]{1,0:T(8,128)S(1)} %dynamic-slice_bitcast_fusion.2, pred[512,512]{0,1:T(8,128)(4,1)S(1)} %broadcast_compare_fusion.5, bf16[2,512,12,64]{1,3,2,0:T(8,128)(2,1)S(1)} %copy-done.8, ...), kind=kOutput, calls=%fused_computation.24.clone.1 | convolution fusion | flops 418375680 | bytes 27059200 | tf_op jit(solution)/shard_map/while/body/eval_jaxpr/qhd,khd->hqk/dot_general | solution.py:275
  257.8 7.1 %multiply_convert_fusion.4 = bf16[12,512,512]{1,2,0:T(8,128)(2,1)S(1)} fusion(f32[12,512,512]{1,2,0:T(8,128)} %get-tuple-element.410, f32[12,512,512]{1,2,0:T(8,128)S(1)} %fusion.149, f32[12,512]{1,0:T(8,128)S(1)} %get-tuple-element.411, f32[12,512]{1,0:T(8,128)S(1)} %dynamic-slice_bitcast_fusion.2, pred[512,512]{0,1:T(8,128)(4,1)S(1)} %broadcast_compare_fusion.5), kind=kLoop, calls=%fused_computation.23.clone.1 | loop fusion | flops 18874368 | bytes 31768576 | tf_op jit(solution)/shard_map/while/body/eval_jaxpr/convert_element_type | solution.py:277
  284.4 4.5 fusion.76
  310.0 7.2 %collective-permute-done.21 = bf16[192,3072]{1,0:T(8,128)(2,1)S(1)} collective-permute-done((bf16[192,3072]{1,0:T(8,128)(2,1)S(1)}, bf16[192,3072]{1,0:T(8,128)(2,1)S(1)}, u32[]{:S(2)}, u32[]{:S(2)}) %collective-permute-start.21) | collective-permute-done | bytes 1179680 | tf_op jit(solution)/shard_map/ppermute | solution.py:84
  319.7 16.4 %collective-permute-done.31 = bf16[768,768]{1,0:T(8,128)(2,1)S(1)} collective-permute-done((bf16[768,768]{1,0:T(8,128)(2,1)S(1)}, bf16[768,768]{1,0:T(8,128)(2,1)S(1)}, u32[]{:S(2)}, u32[]{:S(2)}) %collective-permute-start.31) | collective-permute-done | bytes 1179680 | tf_op jit(solution)/shard_map/ppermute | solution.py:84
  338.6 16.5 %collective-permute-done.6 = bf16[192,3072]{1,0:T(8,128)(2,1)S(1)} collective-permute-done((bf16[192,3072]{1,0:T(8,128)(2,1)S(1)}, bf16[192,3072]{1,0:T(8,128)(2,1)S(1)}, u32[]{:S(2)}, u32[]{:S(2)}) %collective-permute-start.6) | collective-permute-done | bytes 1179680 | tf_op jit(solution)/shard_map/ppermute | solution.py:84
  359.3 6.2 %collective-permute-done.7 = bf16[96,3072]{1,0:T(8,128)(2,1)S(1)} collective-permute-done((bf16[96,3072]{1,0:T(8,128)(2,1)S(1)}, bf16[96,3072]{1,0:T(8,128)(2,1)S(1)}, u32[]{:S(2)}, u32[]{:S(2)}) %collective-permute-start.7) | collective-permute-done | bytes 589856 | tf_op jit(solution)/shard_map/ppermute | solution.py:84
  368.1 9.2 %collective-permute-done.8 = bf16[48,3072]{1,0:T(8,128)(2,1)S(1)} collective-permute-done((bf16[48,3072]{1,0:T(8,128)(2,1)S(1)}, bf16[48,3072]{1,0:T(8,128)(2,1)S(1)}, u32[]{:S(2)}, u32[]{:S(2)}) %collective-permute-start.8) | collective-permute-done | bytes 294944 | tf_op jit(solution)/shard_map/ppermute | solution.py:84
  380.5 11.7 %collective-permute-done.9 = bf16[24,3072]{1,0:T(8,128)(2,1)S(1)} collective-permute-done((bf16[24,3072]{1,0:T(8,128)(2,1)S(1)}, bf16[24,3072]{1,0:T(8,128)(2,1)S(1)}, u32[]{:S(2)}, u32[]{:S(2)}) %collective-permute-start.9) | collective-permute-done | bytes 147488 | tf_op jit(solution)/shard_map/ppermute | solution.py:84
  399.5 6.7 %collective-permute-start.11 = (bf16[48,3072]{1,0:T(8,128)(2,1)S(1)}, bf16[48,3072]{1,0:T(8,128)(2,1)S(1)}, u32[]{:S(2)}, u32[]{:S(2)}) collective-permute-start(bf16[48,3072]{1,0:T(8,128)(2,1)S(1)} %maximum_select_fusion.12), channel_id=1, source_target_pairs={{0,8},{1,9},{2,10},{3,11},{4,12},{5,13},{6,14},{7,15},{8,0},{9,1},... | collective-permute-start | bytes 884744 | tf_op jit(solution)/shard_map/ppermute | solution.py:87
  409.8 7.1 %collective-permute-done.11 = bf16[48,3072]{1,0:T(8,128)(2,1)S(1)} collective-permute-done((bf16[48,3072]{1,0:T(8,128)(2,1)S(1)}, bf16[48,3072]{1,0:T(8,128)(2,1)S(1)}, u32[]{:S(2)}, u32[]{:S(2)}) %collective-permute-start.11) | collective-permute-done | bytes 294944 | tf_op jit(solution)/shard_map/ppermute | solution.py:87
  422.1 4.6 collective-permute-done.36
  449.9 7.0 %collective-permute-done.27 = bf16[96,3072]{1,0:T(8,128)(2,1)S(1)} collective-permute-done((bf16[96,3072]{1,0:T(8,128)(2,1)S(1)}, bf16[96,3072]{1,0:T(8,128)(2,1)S(1)}, u32[]{:S(2)}, u32[]{:S(2)}) %collective-permute-start.27) | collective-permute-done | bytes 589856 | tf_op jit(solution)/shard_map/ppermute | solution.py:87
  475.2 4.1 collective-permute-done.16
  492.0 7.9 %convolution_add_fusion.1 = f32[1024,768]{1,0:T(8,128)} fusion(f32[1024,768]{1,0:T(8,128)S(1)} %copy-done.24, bf16[1024,2304]{0,1:T(8,128)(2,1)} %copy-done.28, bf16[768,2304]{1,0:T(8,128)(2,1)S(1)} %copy-done), kind=kOutput, calls=%fused_computation.145 | convolution fusion | flops 3624665088 | bytes 14548992 | tf_op jit(solution)/shard_map/dot_general | solution.py:368
  504.0 4.6 fusion.73
  513.8 8.6 %fusion.75 = f32[3072,768]{1,0:T(8,128)} fusion(bf16[1536,768]{1,0:T(8,128)(2,1)} %collective-permute-done.39, bf16[1536,768]{1,0:T(8,128)(2,1)} %maximum_select_fusion.5, pred[]{:T(512)S(6)} %eq.88), kind=kLoop, calls=%fused_computation.103 | loop fusion | flops 23592960 | bytes 14155777 | tf_op jit(solution)/shard_map/convert_element_type | solution.py:93
  522.3 9.2 %fusion.74 = f32[768,3072]{1,0:T(8,128)} fusion(bf16[384,3072]{1,0:T(8,128)(2,1)} %collective-permute-done.29, bf16[384,3072]{1,0:T(8,128)(2,1)} %maximum_select_fusion.4, pred[]{:T(512)S(6)} %eq.88), kind=kLoop, calls=%fused_computation.101 | loop fusion | flops 23592960 | bytes 14155777 | tf_op jit(solution)/shard_map/convert_element_type | solution.py:93
  (403 shorter events, 271.7 us)
Async XLA Ops:
  121.7 5.8 %collective-permute-start = (bf16[16,768]{1,0:T(8,128)(2,1)S(1)}, bf16[16,768]{1,0:T(8,128)(2,1)S(1)}, u32[]{:S(2)}, u32[]{:S(2)}) collective-permute-start(bf16[16,768]{1,0:T(8,128)(2,1)S(1)} %get-tuple-element.293.own_ref), channel_id=1, source_target_pairs={{0,16},{1,17},{2,18},{3,19},{4,20},{5,21},{6,22},{7,23},{8,24},{9,... | collective-permute-start | bytes 73736 | tf_op jit(solution)/shard_map/ppermute | solution.py:73
  277.1 20.4 %collective-permute-start.20 = (bf16[384,3072]{1,0:T(8,128)(2,1)}, bf16[384,3072]{1,0:T(8,128)(2,1)}, u32[]{:S(2)}, u32[]{:S(2)}) collective-permute-start(bf16[384,3072]{1,0:T(8,128)(2,1)} %constant_dynamic-slice_fusion.11), channel_id=1, source_target_pairs={{0,1},{1,0},{2,3},{3,2},{4,5},{5,4},{6,7},{7,6},{8,9},{9,8},{10,11... | collective-permute-start | bytes 7077896 | tf_op jit(solution)/shard_map/ppermute | solution.py:84
  279.2 23.8 %collective-permute-start.30 = (bf16[1536,768]{1,0:T(8,128)(2,1)}, bf16[1536,768]{1,0:T(8,128)(2,1)}, u32[]{:S(2)}, u32[]{:S(2)}) collective-permute-start(bf16[1536,768]{1,0:T(8,128)(2,1)} %constant_dynamic-slice_fusion.6), channel_id=1, source_target_pairs={{0,1},{1,0},{2,3},{3,2},{4,5},{5,4},{6,7},{7,6},{8,9},{9,8},{10,11... | collective-permute-start | bytes 7077896 | tf_op jit(solution)/shard_map/ppermute | solution.py:84
  292.5 13.1 %collective-permute-start.5 = (bf16[384,3072]{1,0:T(8,128)(2,1)}, bf16[384,3072]{1,0:T(8,128)(2,1)}, u32[]{:S(2)}, u32[]{:S(2)}) collective-permute-start(bf16[384,3072]{1,0:T(8,128)(2,1)} %fusion.81), channel_id=1, source_target_pairs={{0,1},{1,0},{2,3},{3,2},{4,5},{5,4},{6,7},{7,6},{8,9},{9,8},{10,11... | collective-permute-start | bytes 7077896 | tf_op jit(solution)/shard_map/ppermute | solution.py:84
  300.9 16.3 %collective-permute-start.21 = (bf16[192,3072]{1,0:T(8,128)(2,1)S(1)}, bf16[192,3072]{1,0:T(8,128)(2,1)S(1)}, u32[]{:S(2)}, u32[]{:S(2)}) collective-permute-start(bf16[192,3072]{1,0:T(8,128)(2,1)S(1)} %constant_dynamic-slice_fusion.10), channel_id=1, source_target_pairs={{0,2},{1,5},{2,0},{3,7},{4,6},{5,1},{6,4},{7,3},{8,10},{9,13},{10,... | collective-permute-start | bytes 3538952 | tf_op jit(solution)/shard_map/ppermute | solution.py:84
  305.3 30.8 %collective-permute-start.31 = (bf16[768,768]{1,0:T(8,128)(2,1)S(1)}, bf16[768,768]{1,0:T(8,128)(2,1)S(1)}, u32[]{:S(2)}, u32[]{:S(2)}) collective-permute-start(bf16[768,768]{1,0:T(8,128)(2,1)S(1)} %constant_dynamic-slice_fusion.5), channel_id=1, source_target_pairs={{0,2},{1,5},{2,0},{3,7},{4,6},{5,1},{6,4},{7,3},{8,10},{9,13},{10,... | collective-permute-start | bytes 3538952 | tf_op jit(solution)/shard_map/ppermute | solution.py:84
  308.1 47.0 %collective-permute-start.6 = (bf16[192,3072]{1,0:T(8,128)(2,1)S(1)}, bf16[192,3072]{1,0:T(8,128)(2,1)S(1)}, u32[]{:S(2)}, u32[]{:S(2)}) collective-permute-start(bf16[192,3072]{1,0:T(8,128)(2,1)S(1)} %constant_dynamic-slice_fusion.15), channel_id=1, source_target_pairs={{0,2},{1,5},{2,0},{3,7},{4,6},{5,1},{6,4},{7,3},{8,10},{9,13},{10,... | collective-permute-start | bytes 3538952 | tf_op jit(solution)/shard_map/ppermute | solution.py:84
  317.6 40.0 %collective-permute-start.22 = (bf16[96,3072]{1,0:T(8,128)(2,1)S(1)}, bf16[96,3072]{1,0:T(8,128)(2,1)S(1)}, u32[]{:S(2)}, u32[]{:S(2)}) collective-permute-start(bf16[96,3072]{1,0:T(8,128)(2,1)S(1)} %constant_dynamic-slice_fusion.9), channel_id=1, source_target_pairs={{0,4},{1,3},{2,6},{3,1},{4,0},{5,7},{6,2},{7,5},{8,12},{9,11},{10,... | collective-permute-start | bytes 1769480 | tf_op jit(solution)/shard_map/ppermute | solution.py:84
  336.5 31.2 %collective-permute-start.32 = (bf16[384,768]{1,0:T(8,128)(2,1)S(1)}, bf16[384,768]{1,0:T(8,128)(2,1)S(1)}, u32[]{:S(2)}, u32[]{:S(2)}) collective-permute-start(bf16[384,768]{1,0:T(8,128)(2,1)S(1)} %constant_dynamic-slice_fusion.4), channel_id=1, source_target_pairs={{0,4},{1,3},{2,6},{3,1},{4,0},{5,7},{6,2},{7,5},{8,12},{9,11},{10,... | collective-permute-start | bytes 1769480 | tf_op jit(solution)/shard_map/ppermute | solution.py:84
  355.6 9.9 %collective-permute-start.7 = (bf16[96,3072]{1,0:T(8,128)(2,1)S(1)}, bf16[96,3072]{1,0:T(8,128)(2,1)S(1)}, u32[]{:S(2)}, u32[]{:S(2)}) collective-permute-start(bf16[96,3072]{1,0:T(8,128)(2,1)S(1)} %constant_dynamic-slice_fusion.14), channel_id=1, source_target_pairs={{0,4},{1,3},{2,6},{3,1},{4,0},{5,7},{6,2},{7,5},{8,12},{9,11},{10,... | collective-permute-start | bytes 1769480 | tf_op jit(solution)/shard_map/ppermute | solution.py:84
  357.8 22.5 %collective-permute-start.23 = (bf16[48,3072]{1,0:T(8,128)(2,1)S(1)}, bf16[48,3072]{1,0:T(8,128)(2,1)S(1)}, u32[]{:S(2)}, u32[]{:S(2)}) collective-permute-start(bf16[48,3072]{1,0:T(8,128)(2,1)S(1)} %constant_dynamic-slice_fusion.8), channel_id=1, source_target_pairs={{0,8},{1,9},{2,10},{3,11},{4,12},{5,13},{6,14},{7,15},{8,0},{9,1},... | collective-permute-start | bytes 884744 | tf_op jit(solution)/shard_map/ppermute | solution.py:84
  365.7 11.6 %collective-permute-start.8 = (bf16[48,3072]{1,0:T(8,128)(2,1)S(1)}, bf16[48,3072]{1,0:T(8,128)(2,1)S(1)}, u32[]{:S(2)}, u32[]{:S(2)}) collective-permute-start(bf16[48,3072]{1,0:T(8,128)(2,1)S(1)} %constant_dynamic-slice_fusion.13), channel_id=1, source_target_pairs={{0,8},{1,9},{2,10},{3,11},{4,12},{5,13},{6,14},{7,15},{8,0},{9,1},... | collective-permute-start | bytes 884744 | tf_op jit(solution)/shard_map/ppermute | solution.py:84
  367.9 24.5 %collective-permute-start.33 = (bf16[192,768]{1,0:T(8,128)(2,1)S(1)}, bf16[192,768]{1,0:T(8,128)(2,1)S(1)}, u32[]{:S(2)}, u32[]{:S(2)}) collective-permute-start(bf16[192,768]{1,0:T(8,128)(2,1)S(1)} %constant_dynamic-slice_fusion.3), channel_id=1, source_target_pairs={{0,8},{1,9},{2,10},{3,11},{4,12},{5,13},{6,14},{7,15},{8,0},{9,1},... | collective-permute-start | bytes 884744 | tf_op jit(solution)/shard_map/ppermute | solution.py:84
  377.4 14.9 %collective-permute-start.9 = (bf16[24,3072]{1,0:T(8,128)(2,1)S(1)}, bf16[24,3072]{1,0:T(8,128)(2,1)S(1)}, u32[]{:S(2)}, u32[]{:S(2)}) collective-permute-start(bf16[24,3072]{1,0:T(8,128)(2,1)S(1)} %constant_dynamic-slice_fusion.12), channel_id=1, source_target_pairs={{0,16},{1,17},{2,18},{3,19},{4,20},{5,21},{6,22},{7,23},{8,24},{9,... | collective-permute-start | bytes 442376 | tf_op jit(solution)/shard_map/ppermute | solution.py:84
  380.4 25.7 %collective-permute-start.24 = (bf16[24,3072]{1,0:T(8,128)(2,1)S(1)}, bf16[24,3072]{1,0:T(8,128)(2,1)S(1)}, u32[]{:S(2)}, u32[]{:S(2)}) collective-permute-start(bf16[24,3072]{1,0:T(8,128)(2,1)S(1)} %constant_dynamic-slice_fusion.7), channel_id=1, source_target_pairs={{0,16},{1,17},{2,18},{3,19},{4,20},{5,21},{6,22},{7,23},{8,24},{9,... | collective-permute-start | bytes 442376 | tf_op jit(solution)/shard_map/ppermute | solution.py:84
  392.3 7.1 %collective-permute-start.10 = (bf16[24,3072]{1,0:T(8,128)(2,1)S(1)}, bf16[24,3072]{1,0:T(8,128)(2,1)S(1)}, u32[]{:S(2)}, u32[]{:S(2)}) collective-permute-start(bf16[24,3072]{1,0:T(8,128)(2,1)S(1)} %add_convert_fusion.14), channel_id=1, source_target_pairs={{0,16},{1,17},{2,18},{3,19},{4,20},{5,21},{6,22},{7,23},{8,24},{9,... | collective-permute-start | bytes 442376 | tf_op jit(solution)/shard_map/ppermute | solution.py:87
  392.5 17.1 %collective-permute-start.34 = (bf16[96,768]{1,0:T(8,128)(2,1)S(1)}, bf16[96,768]{1,0:T(8,128)(2,1)S(1)}, u32[]{:S(2)}, u32[]{:S(2)}) collective-permute-start(bf16[96,768]{1,0:T(8,128)(2,1)S(1)} %constant_dynamic-slice_fusion.2), channel_id=1, source_target_pairs={{0,16},{1,17},{2,18},{3,19},{4,20},{5,21},{6,22},{7,23},{8,24},{9,... | collective-permute-start | bytes 442376 | tf_op jit(solution)/shard_map/ppermute | solution.py:84
  399.5 17.4 %collective-permute-start.11 = (bf16[48,3072]{1,0:T(8,128)(2,1)S(1)}, bf16[48,3072]{1,0:T(8,128)(2,1)S(1)}, u32[]{:S(2)}, u32[]{:S(2)}) collective-permute-start(bf16[48,3072]{1,0:T(8,128)(2,1)S(1)} %maximum_select_fusion.12), channel_id=1, source_target_pairs={{0,8},{1,9},{2,10},{3,11},{4,12},{5,13},{6,14},{7,15},{8,0},{9,1},... | collective-permute-start | bytes 884744 | tf_op jit(solution)/shard_map/ppermute | solution.py:87
  406.2 15.1 %collective-permute-start.25 = (bf16[24,3072]{1,0:T(8,128)(2,1)S(1)}, bf16[24,3072]{1,0:T(8,128)(2,1)S(1)}, u32[]{:S(2)}, u32[]{:S(2)}) collective-permute-start(bf16[24,3072]{1,0:T(8,128)(2,1)S(1)} %add_convert_fusion.13), channel_id=1, source_target_pairs={{0,16},{1,17},{2,18},{3,19},{4,20},{5,21},{6,22},{7,23},{8,24},{9,... | collective-permute-start | bytes 442376 | tf_op jit(solution)/shard_map/ppermute | solution.py:87
  409.7 10.1 %collective-permute-start.35 = (bf16[96,768]{1,0:T(8,128)(2,1)S(1)}, bf16[96,768]{1,0:T(8,128)(2,1)S(1)}, u32[]{:S(2)}, u32[]{:S(2)}) collective-permute-start(bf16[96,768]{1,0:T(8,128)(2,1)S(1)} %add_convert_fusion.12), channel_id=1, source_target_pairs={{0,16},{1,17},{2,18},{3,19},{4,20},{5,21},{6,22},{7,23},{8,24},{9,... | collective-permute-start | bytes 442376 | tf_op jit(solution)/shard_map/ppermute | solution.py:87
  417.0 14.6 %collective-permute-start.12 = (bf16[96,3072]{1,0:T(8,128)(2,1)S(1)}, bf16[96,3072]{1,0:T(8,128)(2,1)S(1)}, u32[]{:S(2)}, u32[]{:S(2)}) collective-permute-start(bf16[96,3072]{1,0:T(8,128)(2,1)S(1)} %maximum_select_fusion.9), channel_id=1, source_target_pairs={{0,4},{1,3},{2,6},{3,1},{4,0},{5,7},{6,2},{7,5},{8,12},{9,11},{10,... | collective-permute-start | bytes 1769480 | tf_op jit(solution)/shard_map/ppermute | solution.py:87
  419.9 6.8 %collective-permute-start.36 = (bf16[192,768]{1,0:T(8,128)(2,1)S(1)}, bf16[192,768]{1,0:T(8,128)(2,1)S(1)}, u32[]{:S(2)}, u32[]{:S(2)}) collective-permute-start(bf16[192,768]{1,0:T(8,128)(2,1)S(1)} %maximum_select_fusion.14), channel_id=1, source_target_pairs={{0,8},{1,9},{2,10},{3,11},{4,12},{5,13},{6,14},{7,15},{8,0},{9,1},... | collective-permute-start | bytes 884744 | tf_op jit(solution)/shard_map/ppermute | solution.py:87
  421.3 14.4 %collective-permute-start.26 = (bf16[48,3072]{1,0:T(8,128)(2,1)S(1)}, bf16[48,3072]{1,0:T(8,128)(2,1)S(1)}, u32[]{:S(2)}, u32[]{:S(2)}) collective-permute-start(bf16[48,3072]{1,0:T(8,128)(2,1)S(1)} %maximum_select_fusion.13), channel_id=1, source_target_pairs={{0,8},{1,9},{2,10},{3,11},{4,12},{5,13},{6,14},{7,15},{8,0},{9,1},... | collective-permute-start | bytes 884744 | tf_op jit(solution)/shard_map/ppermute | solution.py:87
  426.8 17.4 %collective-permute-start.37 = (bf16[384,768]{1,0:T(8,128)(2,1)S(1)}, bf16[384,768]{1,0:T(8,128)(2,1)S(1)}, u32[]{:S(2)}, u32[]{:S(2)}) collective-permute-start(bf16[384,768]{1,0:T(8,128)(2,1)S(1)} %maximum_select_fusion.11), channel_id=1, source_target_pairs={{0,4},{1,3},{2,6},{3,1},{4,0},{5,7},{6,2},{7,5},{8,12},{9,11},{10,... | collective-permute-start | bytes 1769480 | tf_op jit(solution)/shard_map/ppermute | solution.py:87
  431.9 31.4 %collective-permute-start.13 = (bf16[192,3072]{1,0:T(8,128)(2,1)S(1)}, bf16[192,3072]{1,0:T(8,128)(2,1)S(1)}, u32[]{:S(2)}, u32[]{:S(2)}) collective-permute-start(bf16[192,3072]{1,0:T(8,128)(2,1)S(1)} %maximum_select_fusion.6), channel_id=1, source_target_pairs={{0,2},{1,5},{2,0},{3,7},{4,6},{5,1},{6,4},{7,3},{8,10},{9,13},{10,... | collective-permute-start | bytes 3538952 | tf_op jit(solution)/shard_map/ppermute | solution.py:87
  435.9 21.0 %collective-permute-start.27 = (bf16[96,3072]{1,0:T(8,128)(2,1)S(1)}, bf16[96,3072]{1,0:T(8,128)(2,1)S(1)}, u32[]{:S(2)}, u32[]{:S(2)}) collective-permute-start(bf16[96,3072]{1,0:T(8,128)(2,1)S(1)} %maximum_select_fusion.10), channel_id=1, source_target_pairs={{0,4},{1,3},{2,6},{3,1},{4,0},{5,7},{6,2},{7,5},{8,12},{9,11},{10,... | collective-permute-start | bytes 1769480 | tf_op jit(solution)/shard_map/ppermute | solution.py:87
  444.7 23.0 %collective-permute-start.38 = (bf16[768,768]{1,0:T(8,128)(2,1)S(1)}, bf16[768,768]{1,0:T(8,128)(2,1)S(1)}, u32[]{:S(2)}, u32[]{:S(2)}) collective-permute-start(bf16[768,768]{1,0:T(8,128)(2,1)S(1)} %maximum_select_fusion.8), channel_id=1, source_target_pairs={{0,2},{1,5},{2,0},{3,7},{4,6},{5,1},{6,4},{7,3},{8,10},{9,13},{10,... | collective-permute-start | bytes 3538952 | tf_op jit(solution)/shard_map/ppermute | solution.py:87
  458.1 25.4 %collective-permute-start.28 = (bf16[192,3072]{1,0:T(8,128)(2,1)}, bf16[192,3072]{1,0:T(8,128)(2,1)}, u32[]{:S(2)}, u32[]{:S(2)}) collective-permute-start(bf16[192,3072]{1,0:T(8,128)(2,1)} %maximum_select_fusion.7), channel_id=1, source_target_pairs={{0,2},{1,5},{2,0},{3,7},{4,6},{5,1},{6,4},{7,3},{8,10},{9,13},{10,... | collective-permute-start | bytes 3538952 | tf_op jit(solution)/shard_map/ppermute | solution.py:87
  465.1 38.9 %collective-permute-start.14 = (bf16[384,3072]{1,0:T(8,128)(2,1)}, bf16[384,3072]{1,0:T(8,128)(2,1)}, u32[]{:S(2)}, u32[]{:S(2)}) collective-permute-start(bf16[384,3072]{1,0:T(8,128)(2,1)} %maximum_select_fusion.3), channel_id=1, source_target_pairs={{0,1},{1,0},{2,3},{3,2},{4,5},{5,4},{6,7},{7,6},{8,9},{9,8},{10,11... | collective-permute-start | bytes 7077896 | tf_op jit(solution)/shard_map/ppermute | solution.py:87
  469.5 44.3 %collective-permute-start.39 = (bf16[1536,768]{1,0:T(8,128)(2,1)}, bf16[1536,768]{1,0:T(8,128)(2,1)}, u32[]{:S(2)}, u32[]{:S(2)}) collective-permute-start(bf16[1536,768]{1,0:T(8,128)(2,1)} %maximum_select_fusion.5), channel_id=1, source_target_pairs={{0,1},{1,0},{2,3},{3,2},{4,5},{5,4},{6,7},{7,6},{8,9},{9,8},{10,11... | collective-permute-start | bytes 7077896 | tf_op jit(solution)/shard_map/ppermute | solution.py:87
  487.4 34.9 %collective-permute-start.29 = (bf16[384,3072]{1,0:T(8,128)(2,1)}, bf16[384,3072]{1,0:T(8,128)(2,1)}, u32[]{:S(2)}, u32[]{:S(2)}) collective-permute-start(bf16[384,3072]{1,0:T(8,128)(2,1)} %maximum_select_fusion.4), channel_id=1, source_target_pairs={{0,1},{1,0},{2,3},{3,2},{4,5},{5,4},{6,7},{7,6},{8,9},{9,8},{10,11... | collective-permute-start | bytes 7077896 | tf_op jit(solution)/shard_map/ppermute | solution.py:87
  488.8 12.4 %collective-permute-start.19 = (f32[12,768]{1,0:T(8,128)S(1)}, f32[12,768]{1,0:T(8,128)S(1)}, u32[]{:S(2)}, u32[]{:S(2)}) collective-permute-start(f32[12,768]{1,0:T(8,128)S(1)} %add.308), channel_id=1, source_target_pairs={{0,16},{1,17},{2,18},{3,19},{4,20},{5,21},{6,22},{7,23},{8,24},{9,... | collective-permute-start | bytes 110600 | tf_op jit(solution)/shard_map/ppermute | solution.py:99
  (95 other events, 736.0 us)
